TPU v7x, 32 devices: a whole 2x2x4 slice. The times are simulated.
32 devices in a mesh: table: 16 (over z, y, core), rep: 2 (over x).
Axes of the slice: x: 2, y: 2, z: 4, core: 2. Of those that a mesh axis runs over, the one named last changes fastest.
Arguments:
- bag_rows: int32 [32, 1024, 8], P(('table', 'rep')), may hold values from 0 to 2047
- bag_owner: int32 [32, 1024, 8], P(('table', 'rep')), may hold values from 0 to 15, all different within a row; in each aligned block of 1024 rows (0 to 1023, 1024 to 2047, ..., all dimensions but the last counted through in order) at most 768 rows name the same one
- bag_weight: float32 [32, 1024, 8], P(('table', 'rep')), may hold values from 0.25 to 2
- tables: bfloat16 [4, 32768, 128], P(None, 'table'), may hold values from -3 to 3
- returning: int32 [32], P(('table', 'rep')), may hold values 0 or 1
- home: int32 [32], P(('table', 'rep')), may hold values from 0 to 1
- entry: int32 [32], P(('table', 'rep')), may hold values from 0 to 7
- stores: bfloat16 [256, 30, 512], P(('table', 'rep')), may hold values from -6 to 6
- conv_weight: bfloat16 [4, 1536, 512], P(None, 'table'), may hold values from -0.15625 to 0.15625
- norm_gain: float32 [4, 512], replicated, may hold values from 0.1 to 1.9
Outputs:
- hidden: bfloat16 [32, 1024, 512], P(('table', 'rep'))
Inputs may be any that keep to these rules, and one draw needn't show every extreme that they name: `bag_owner`: the 8 ids of one slot name different owners. Among the slots of one device no owner is named by more than 768 ids, and in some devices' slots one owner is named by exactly 768.
All inputs are finite; a program needn't handle non-finite values. No bound on the sum of `returning` on one device may be relied on, other than what follows from the above.
Results may differ from a plain program's by a relative error of at most 0.0057.
Values may be sent and summed in bfloat16 or wider, within the bound.
No kernel may reach another device: no remote copies, remote signals or barrier semaphores. Data moves between devices by JAX's collectives and lax.ppermute only.
A program may use at most 64 MiB of HBM per device.

v0:
```python
import jax
import jax.numpy as jnp
from jax import lax
from jax.sharding import PartitionSpec as P

table_of_id = (0, 1, 2, 2, 3, 3, 3, 3)
bag_bounds = ((0, 1), (1, 2), (2, 4), (4, 8))
epsilon = 1e-05


def pool_bags(weighted):
    sums = [jnp.sum(weighted[..., lower:upper, :], axis=-2) for lower, upper in bag_bounds]
    return jnp.concatenate(sums, axis=-1)


def norm_relu(values, gain):
    mean = jnp.mean(values, axis=-1, keepdims=True)
    centred = values - mean
    spread = jnp.mean(centred * centred, axis=-1, keepdims=True)
    return jnp.maximum(centred * lax.rsqrt(spread + epsilon) * gain, 0.0)


def stack_taps(inputs, carried, offset, dilation):
    span = 2 * dilation
    extended = jnp.concatenate([carried[..., offset : offset + span, :], inputs], axis=-2)
    length = inputs.shape[-2]
    taps = [
        extended[..., span - tap * dilation : span - tap * dilation + length, :] for tap in range(3)
    ]
    return jnp.concatenate(taps, axis=-1)


def local(
    bag_rows, bag_owner, bag_weight, tables, returning, home, entry, stores, conv_weight, norm_gain
):
    owners = lax.axis_size("table")
    samples_here, slot_count, bag_width = bag_rows.shape
    token_count = samples_here * slot_count
    shard_rows = tables.shape[1]
    row_width = tables.shape[2]
    flat_owner = bag_owner.reshape(token_count * bag_width)
    local_rows = (jnp.array(table_of_id, jnp.int32)[None, None, :] * shard_rows + bag_rows).reshape(
        token_count * bag_width
    )
    capacity = min(token_count, (3 * token_count * bag_width + 2 * owners - 1) // (2 * owners))
    onehot = (flat_owner[:, None] == jnp.arange(owners, dtype=jnp.int32)[None, :]).astype(jnp.int32)
    earlier = jnp.cumsum(onehot, axis=0) - onehot
    ranking = jnp.sum(earlier * onehot, axis=1)
    placed = flat_owner * capacity + ranking
    requests = (
        jnp.zeros((owners * capacity,), jnp.int32)
        .at[placed]
        .set(local_rows)
        .reshape(owners, capacity)
    )
    flat_table = tables.reshape(-1, row_width)
    received = lax.all_to_all(requests, "table", split_axis=0, concat_axis=0, tiled=True)
    returned = lax.all_to_all(
        flat_table[received], "table", split_axis=0, concat_axis=0, tiled=True
    )
    picked = returned.reshape(owners * capacity, row_width)[placed].astype(jnp.float32)
    picked = picked * bag_weight.reshape(-1)[:, None]
    block_in = pool_bags(picked.reshape(samples_here, slot_count, bag_width, row_width)).astype(
        jnp.bfloat16
    )
    collected = lax.all_gather(stores, "rep", axis=0, tiled=True)
    carried = collected[home * stores.shape[0] + entry]
    carried = jnp.where(returning[:, None, None] > 0, carried, jnp.zeros_like(carried))
    channels = conv_weight.shape[-1]
    inputs = block_in
    offset = 0
    for layer in range(conv_weight.shape[0]):
        dilation = 2**layer
        stacked = stack_taps(inputs, carried, offset, dilation).reshape(token_count, 3 * channels)
        output = jnp.dot(
            stacked,
            lax.all_gather(conv_weight[layer], "table", axis=0, tiled=True),
            preferred_element_type=jnp.float32,
        )
        active = norm_relu(output, norm_gain[layer]).reshape(samples_here, slot_count, channels)
        offset = offset + 2 * dilation
        if layer % 2 == 0:
            inputs = active.astype(jnp.bfloat16)
        else:
            block_in = (active + block_in.astype(jnp.float32)).astype(jnp.bfloat16)
            inputs = block_in
    return block_in


def solution(mesh):
    in_specs = (
        P(("table", "rep"), None, None),
        P(("table", "rep"), None, None),
        P(("table", "rep"), None, None),
        P(None, "table", None),
        P(("table", "rep")),
        P(("table", "rep")),
        P(("table", "rep")),
        P(("table", "rep"), None, None),
        P(None, "table", None),
        P(),
    )
    out_specs = P(("table", "rep"), None, None)
    return jax.shard_map(local, mesh=mesh, in_specs=in_specs, out_specs=out_specs, check_vma=False)
```

profile of v0, /device:TPU:15, one launch (start us, length us, event | category | flops | bytes accessed | tf_op | source)
XLA Modules:
  0.0 271.7 jit_solution(2655229296490653989)
XLA Ops:
  6.5 1.9 fusion.51
  8.5 0.7 all-gather.11.cloned.1.call-update
  9.2 1.0 copy.22
  10.2 0.3 eq.29
  10.5 0.3 eq.25
  10.8 4.8 %reduce-window.6 = s32[16,64,128]{2,1,0:T(8,128)S(1)} reduce-window(s32[16,64,128]{2,1,0:T(8,128)S(1)} %fusion.39, s32[]{:T(128)} %constant.13.clone.1), window={size=1x1x128 pad=0_0x0_0x127_0}, to_apply=%region_0.0 | reduce-window | flops 16646144 | bytes 1048580 | tf_op jit(solution)/shard_map/reduce-window
  15.6 0.5 slice_reduce_fusion.2
  16.1 0.2 reduce-window.9
  16.7 0.3 mul.127
  17.0 0.4 fusion.38
  17.8 0.3 reshape.328
  18.1 30.5 %scatter_custom_fusion = s32[12288]{0:T(1024)S(1)} fusion(s32[8192]{0:T(1024)S(1)} %bitcast.108, s32[8192]{0:T(1024)S(1)} %reshape.328, s32[]{:T(128)} %constant.13.clone.1), kind=kCustom, calls=%fused_computation.79 | custom fusion | bytes 49156 | tf_op jit(solution)/shard_map/scatter | solution.py:53
  48.5 10.6 %all_to_all.17 = s32[16,1,768]{2,1,0:T(1,128)S(1)} all-to-all(s32[16,1,768]{2,1,0:T(1,128)S(1)} %bitcast.105), channel_id=1, replica_groups=mesh['table'=16,'rep'=2] {'table'}, dimensions={0} | all-to-all | bytes 98304 | tf_op jit(solution)/shard_map/all_to_all | solution.py:57
  59.2 43.3 %gather_fusion = bf16[12288,128]{1,0:T(8,128)(2,1)} fusion(bf16[8192,128]{1,0:T(8,128)(2,1)S(1)} %bitcast.98, s32[12288]{0:T(1024)S(1)} %broadcast_clamp_fusion), kind=kCustom, calls=%fused_computation | custom fusion | bytes 6340608 | tf_op jit(solution)/shard_map/gather | solution.py:59
  102.5 7.0 %all-to-all-start.1 = ((bf16[16,768,128]{2,1,0:T(8,128)(2,1)}), bf16[16,768,128]{2,1,0:T(8,128)(2,1)}, u32[]{:S(2)}, u32[]{:S(2)}) async-start(bf16[16,768,128]{2,1,0:T(8,128)(2,1)} %bitcast.99), calls=%async_computation.1 | async-start | bytes 6291456 | tf_op jit(solution)/shard_map/all_to_all | solution.py:58
  109.5 0.7 all-gather.13.cloned.1.call-update
  110.3 0.5 all-gather.15.cloned.1.call-update
  112.8 8.0 %all_gather.15 = bf16[16,30,512]{2,0,1:T(8,128)(2,1)S(1)} all-gather(bf16[8,30,512]{2,0,1:T(8,128)(2,1)S(1)} %copy-done.6), channel_id=1, replica_groups=mesh['table'=16,'rep'=2] {'rep'}, dimensions={0}, use_global_device_ids=true | all-gather | bytes 737280 | tf_op jit(solution)/shard_map/all_gather | solution.py:66
  120.9 68.1 %all-to-all-done.1 = bf16[16,768,128]{2,1,0:T(8,128)(2,1)} async-done(((bf16[16,768,128]{2,1,0:T(8,128)(2,1)}), bf16[16,768,128]{2,1,0:T(8,128)(2,1)}, u32[]{:S(2)}, u32[]{:S(2)}) %all-to-all-start.1) | async-done | bytes 3145760 | tf_op jit(solution)/shard_map/all_to_all | solution.py:58
  189.0 30.5 %gather_fusion.1 = bf16[8192,128]{1,0:T(8,128)(2,1)} fusion(bf16[12288,128]{1,0:T(8,128)(2,1)} %bitcast.8, s32[8192]{0:T(1024)S(1)} %broadcast_clamp_fusion.1), kind=kCustom, calls=%fused_computation.1 | custom fusion | bytes 4227072 | tf_op jit(solution)/shard_map/gather | solution.py:61
  219.5 1.9 bitcast_convert_fusion
  221.4 1.1 copy_multiply_fusion
  222.5 0.9 constant_dynamic-update-slice_fusion.3
  223.6 0.9 copy-done.2
  224.5 0.8 constant_dynamic-update-slice_fusion.2
  225.3 0.8 constant_dynamic-update-slice_fusion.1
  226.1 0.8 constant_dynamic-update-slice_fusion
  226.9 0.4 maximum_maximum_fusion
  227.3 1.3 slice_dynamic-update-slice_fusion.1
  228.6 1.2 slice_dynamic-update-slice_fusion
  229.8 4.2 %fusion.53 = (f32[1024]{0:T(1024)S(1)}, f32[1024,512]{1,0:T(8,128)S(1)}) fusion(bf16[1,1536,512]{2,1,0:T(8,128)(2,1)} %all-gather.9.cloned.1.call-done, bf16[1,1024,1536]{2,1,0:T(8,128)(2,1)} %slice_dynamic-update-slice_fusion), kind=kOutput, calls=%fused_computation.102 | convolution fusion | flops 1611136000 | bytes 6819840 | tf_op jit(solution)/shard_map/dot_general | solution.py:75
  234.0 0.4 multiply_reduce_fusion.3
  234.5 0.4 fusion.33
  234.8 1.2 fusion.31
  236.1 3.7 %fusion.54 = (f32[1024]{0:T(1024)S(1)}, f32[1024,512]{1,0:T(8,128)S(1)}) fusion(bf16[1,1536,512]{2,1,0:T(8,128)(2,1)} %all-gather.11.cloned.1.call-done, bf16[1,1024,512]{2,1,0:T(8,128)(2,1)S(1)} %fusion.33, bf16[1,4,512]{2,1,0:T(4,128)(2,1)S(1)} %slice.126, bf16[1,1024,512]{2,1,0:T(8,128)(2,1)} %fusion.31), kind=kOutput, calls=%fused_computation.103 | convolution fusion | flops 1623718912 | bytes 5775360 | tf_op jit(solution)/shard_map/dot_general | solution.py:75
  239.8 0.4 multiply_reduce_fusion.2
  240.3 1.3 fusion.40
  241.5 0.8 add_convert_fusion.1
  242.4 1.2 fusion.30
  243.6 6.4 %fusion.55 = (f32[1024]{0:T(1024)S(1)}, f32[1024,512]{1,0:T(8,128)S(1)}) fusion(bf16[1,1536,512]{2,1,0:T(8,128)(2,1)} %all-gather.13.cloned.1.call-done, bf16[1,1024,512]{2,1,0:T(8,128)(2,1)S(1)} %bitcast.101, bf16[1,8,512]{2,1,0:T(8,128)(2,1)S(1)} %slice.129, bf16[1,1024,512]{2,1,0:T(8,128)(2,1)} %fusion.30), kind=kOutput, calls=%fused_computation.104 | convolution fusion | flops 1623718912 | bytes 5779456 | tf_op jit(solution)/shard_map/dot_general | solution.py:75
  250.0 0.4 multiply_reduce_fusion.1
  250.5 0.4 fusion.34
  250.9 1.0 copy-done.3
  251.8 1.1 fusion.32
  252.9 5.7 %fusion.56 = (f32[1024]{0:T(1024)S(1)}, f32[1024,512]{0,1:T(8,128)}) fusion(bf16[1,1536,512]{2,1,0:T(8,128)(2,1)} %all-gather.15.cloned.1.call-done, bf16[1,1024,512]{2,1,0:T(8,128)(2,1)} %copy-done.3, bf16[1,16,512]{2,1,0:T(8,128)(2,1)S(1)} %slice.132, bf16[1,1024,512]{2,1,0:T(8,128)(2,1)} %fusion.32), kind=kOutput, calls=%fused_computation.105 | convolution fusion | flops 1623718912 | bytes 5787648 | tf_op jit(solution)/shard_map/dot_general | solution.py:75
  258.5 2.9 %copy.27 = f32[1024,512]{1,0:T(8,128)} copy(f32[1024,512]{0,1:T(8,128)} %get-tuple-element.37) | data formatting | bytes 4194304 | tf_op jit(solution)/shard_map/dot_general | solution.py:75
  261.4 2.1 multiply_reduce_fusion
  263.6 1.5 fusion.35
  (58 shorter events, 1.4 us)
Async XLA Ops:
  6.5 52.6 %copy-start = (bf16[4,2048,128]{2,1,0:T(8,128)(2,1)S(1)}, bf16[4,2048,128]{2,1,0:T(8,128)(2,1)}, u32[]{:S(2)}) copy-start(bf16[4,2048,128]{2,1,0:T(8,128)(2,1)} %param.14) | copy-start | bytes 6291460
  6.5 4.2 %copy-start.7 = (s32[1,1024,8]{1,2,0:T(8,128)S(1)}, s32[1,1024,8]{1,2,0:T(8,128)}, u32[]{:S(2)}) copy-start(s32[1,1024,8]{1,2,0:T(8,128)} %param.12) | copy-start | bytes 98308
  6.5 223.2 %all-gather.9.cloned.1.call-start = ((), (), s32[]{:S(2)}) async-start(), calls=%async_computation.2 | async-start | bytes 1671168 | tf_op jit(solution)/shard_map/all_gather | solution.py:77
  8.5 227.6 %all-gather.11.cloned.1.call-start = ((), (), s32[]{:S(2)}) async-start(), calls=%async_computation.3 | async-start | bytes 1671168 | tf_op jit(solution)/shard_map/all_gather | solution.py:77
  10.8 6.7 %copy-start.9 = (s32[1,1024,8]{1,2,0:T(8,128)S(1)}, s32[1,1024,8]{1,2,0:T(8,128)}, u32[]{:S(2)}) copy-start(s32[1,1024,8]{1,2,0:T(8,128)} %param.11) | copy-start | bytes 98308
  10.8 6.7 %copy-start.11 = (s32[8]{0:T(128)S(1)}, s32[8]{0:T(128)}, u32[]{:S(2)}) copy-start(s32[8]{0:T(128)} %constant.71) | copy-start | bytes 100
  102.5 10.3 %copy-start.6 = (bf16[8,30,512]{2,0,1:T(8,128)(2,1)S(1)}, bf16[8,30,512]{2,0,1:T(8,128)(2,1)}, u32[]{:S(2)}) copy-start(bf16[8,30,512]{2,0,1:T(8,128)(2,1)} %param.18) | copy-start | bytes 737284
  102.5 18.4 %copy-start.10 = (f32[4,512]{1,0:T(4,128)S(1)}, f32[4,512]{1,0:T(4,128)}, u32[]{:S(2)}) copy-start(f32[4,512]{1,0:T(4,128)} %param.20) | copy-start | bytes 24580
  102.5 86.5 %all-to-all-start.1 = ((bf16[16,768,128]{2,1,0:T(8,128)(2,1)}), bf16[16,768,128]{2,1,0:T(8,128)(2,1)}, u32[]{:S(2)}, u32[]{:S(2)}) async-start(bf16[16,768,128]{2,1,0:T(8,128)(2,1)} %bitcast.99), calls=%async_computation.1 | async-start | bytes 6291456 | tf_op jit(solution)/shard_map/all_to_all | solution.py:58
  109.5 134.1 %all-gather.13.cloned.1.call-start = ((), (), s32[]{:S(2)}) async-start(), calls=%async_computation.4 | async-start | bytes 1671168 | tf_op jit(solution)/shard_map/all_gather | solution.py:77
  110.2 142.6 %all-gather.15.cloned.1.call-start = ((), (), s32[]{:S(2)}) async-start(), calls=%async_computation.5 | async-start | bytes 1671168 | tf_op jit(solution)/shard_map/all_gather | solution.py:77
  219.5 1.9 copy-start.8
  222.5 2.0 copy-start.2
  223.6 5.1 %copy-start.4 = (bf16[1024,128]{1,0:T(8,128)(2,1)}, bf16[1024,128]{1,0:T(8,128)(2,1)S(1)}, u32[]{:S(2)}) copy-start(bf16[1024,128]{1,0:T(8,128)(2,1)S(1)} %slice_reduce_fusion) | copy-start | bytes 786436
  239.8 1.7 copy-start.5
  250.8 1.0 copy-start.3
  261.4 2.2 copy-start.1
Sparse Core Ops, SparseCore 0:
  9.6 39.6 all-gather.8
  51.6 38.5 all-gather.10
  112.6 66.6 all-gather.12
  181.5 45.0 all-gather.14
where the time goes:
time: 272 us
  local copies, waits for them, and re-layouts  121 us (44%)
  waiting for transfers between devices  70 us (26%)
  matrix products  20 us (7%)
  other arithmetic  19.5 us (7%)
  blocking collectives  18.5 us (7%)
  between operations  15.5 us (6%)
  starting transfers between devices  7.15 us (3%)
    all_to_all x1, waiting for transfers between devices, local(): lax.all_to_all(flat_table[received], 'table', split_axis=0, concat_axis=0...  68.1 us
    gather x1, local copies, waits for them, and re-layouts, local(): flat_table[received]  43.3 us
    scatter x1, local copies, waits for them, and re-layouts, local(): requests = jnp.zeros((owners * capacity,), jnp.int32).at[placed].set(loca...  30.5 us
    gather x1, local copies, waits for them, and re-layouts, local(): returned.reshape(owners * capacity, row_width)[placed].astype(jnp.float32)  30.5 us
    dot_general x4, matrix products, local(): jnp.dot(stacked, lax.all_gather(conv_weight[layer], 'table', axis=0, tile...  20 us
    all_to_all x1, blocking collectives, local(): lax.all_to_all(requests, 'table', split_axis=0, concat_axis=0, tiled=True)  10.6 us
    all_gather x1, blocking collectives, local(): collected = lax.all_gather(stores, 'rep', axis=0, tiled=True)  7.96 us
    unnamed x30, local copies, waits for them, and re-layouts  7.52 us
  transfers between devices with their start and end apart: 5, of which 1 were waited for; matrix products, arithmetic and copies ran while one was open for 53% of the time, Pallas kernels for 0%

commit v1 on v0

v1 whole, which is shorter than its diff:
```python
import functools
import jax
import jax.numpy as jnp
from jax import lax
from jax.experimental import pallas as pl
from jax.experimental.pallas import tpu as pltpu
from jax.sharding import PartitionSpec as P

table_of_id = (0, 1, 2, 2, 3, 3, 3, 3)
bag_bounds = ((0, 1), (1, 2), (2, 4), (4, 8))
epsilon = 1e-05
parts = 3
unroll = 16
vmem_bytes = 48 * 1024 * 1024


def prep_kernel(piece, shard_rows, rows_ref, owner_ref, request_ref, place_ref):
    owner = owner_ref[...]
    rows = rows_ref[...]
    owners = request_ref.shape[0]
    width, slots = owner.shape
    value_bits = (len(bag_bounds) * shard_rows).bit_length()
    owner_ids = lax.broadcasted_iota(jnp.int32, (owners, slots), 0)
    lane = lax.broadcasted_iota(jnp.int32, (owners, slots), 1)
    value = jnp.zeros((owners, slots), jnp.int32)
    for k in range(width):
        named = owner[k : k + 1, :] == owner_ids
        value = jnp.where(named, rows[k : k + 1, :] + (table_of_id[k] * shard_rows + 1), value)
    present = jnp.where(value > 0, 1, 0)
    rank = present
    step = 1
    while step < slots:
        rank = rank + jnp.where(lane >= step, pltpu.roll(rank, step, 1), 0)
        step *= 2
    rank = rank - present
    place = jnp.zeros((width, slots), jnp.int32)
    for number in range(owners):
        place = jnp.where(owner == number, rank[number : number + 1, :], place)
    part = jnp.zeros((width, slots), jnp.int32)
    for number in range(1, parts):
        part = part + jnp.where(place >= number * piece, 1, 0)
    place_ref[...] = part * ((owners - 1) * piece) + owner * piece + place
    packed = jnp.where(value > 0, ((lane - rank) << value_bits) + value, 0)
    step = 1
    level = value_bits
    while step < slots:
        moving = jnp.where(((packed >> level) & 1) == 1, packed, 0)
        packed = (packed - moving) + pltpu.roll(moving, slots - step, 1)
        step *= 2
        level += 1
    value = jnp.maximum((packed & ((1 << value_bits) - 1)) - 1, 0)
    request_ref[...] = value[:, : request_ref.shape[1]]


def gather_kernel(first, piece, index_ref, table_ref, out_ref, scratch):
    owners = index_ref.shape[0]

    def one_owner(number, carry):
        def some_rows(block, inner):
            base = block * unroll
            for i in range(unroll):
                row = index_ref[number, first + base + i]
                scratch[pl.ds(base + i, 1), :] = table_ref[pl.ds(row, 1), :]
            return inner

        lax.fori_loop(0, piece // unroll, some_rows, 0)
        out_ref[number] = scratch[...].astype(jnp.bfloat16)
        return carry

    lax.fori_loop(0, owners, one_owner, 0)


def pool_kernel(place_ref, weight_ref, *refs):
    piece_refs = refs[:parts]
    out_ref, table, picked = refs[parts:]
    count = piece_refs[0].shape[0]
    for number in range(parts):
        table[number * count : (number + 1) * count, :] = piece_refs[number][...].astype(jnp.float32)
    width, slots, lanes = picked.shape
    block = 8

    def some_slots(step, carry):
        base = step * block
        for k in range(width):
            for i in range(block):
                row = place_ref[k, base + i]
                picked[k, pl.ds(base + i, 1), :] = table[pl.ds(row, 1), :]
        return carry

    lax.fori_loop(0, slots // block, some_slots, 0)
    for t, (lower, upper) in enumerate(bag_bounds):
        total = picked[lower] * weight_ref[:, lower : lower + 1]
        for k in range(lower + 1, upper):
            total = total + picked[k] * weight_ref[:, k : k + 1]
        out_ref[:, t * lanes : (t + 1) * lanes] = total.astype(jnp.bfloat16)


def conv_kernel(pooled_ref, carried_ref, weight_ref, gain_ref, out_ref, first_buf, second_buf):
    front = 16
    rows = 256
    slots = pooled_ref.shape[0]
    layers = weight_ref.shape[0]
    first_buf[front:, :] = pooled_ref[...].astype(jnp.float32)
    offset = 0
    for layer in range(layers):
        dilation = 2**layer
        span = 2 * dilation
        source, target = (first_buf, second_buf) if layer % 2 == 0 else (second_buf, first_buf)
        source[front - span : front, :] = carried_ref[offset : offset + span, :]
        offset += span
        for block in range(slots // rows):
            base = front + block * rows
            taps = [
                source[base - tap * dilation : base - tap * dilation + rows, :].astype(jnp.bfloat16)
                for tap in range(3)
            ]
            output = jnp.dot(
                jnp.concatenate(taps, axis=1), weight_ref[layer], preferred_element_type=jnp.float32
            )
            mean = jnp.mean(output, axis=-1, keepdims=True)
            centred = output - mean
            spread = jnp.mean(centred * centred, axis=-1, keepdims=True)
            active = jnp.maximum(
                centred * lax.rsqrt(spread + epsilon) * gain_ref[layer : layer + 1, :], 0.0
            )
            if layer % 2 == 1:
                active = active + target[base : base + rows, :]
            active = active.astype(jnp.bfloat16)
            if layer == layers - 1:
                out_ref[block * rows : (block + 1) * rows, :] = active
            else:
                target[base : base + rows, :] = active.astype(jnp.float32)


def local(
    bag_rows, bag_owner, bag_weight, tables, returning, home, entry, stores, conv_weight, norm_gain
):
    owners = lax.axis_size("table")
    copies = lax.axis_size("rep")
    samples_here, slot_count, bag_width = bag_rows.shape
    token_count = samples_here * slot_count
    shard_rows = tables.shape[1]
    row_width = tables.shape[2]
    channels = conv_weight.shape[-1]
    capacity = min(token_count, (3 * token_count * bag_width + 2 * owners - 1) // (2 * owners))
    piece = capacity // parts
    params = pltpu.CompilerParams(vmem_limit_bytes=vmem_bytes)
    smem = pl.BlockSpec(memory_space=pltpu.SMEM)
    vmem = pl.BlockSpec(memory_space=pltpu.VMEM)

    weights = lax.all_gather(conv_weight, "table", axis=1, tiled=True)

    rows_by_slot = bag_rows.reshape(token_count, bag_width).T
    owner_by_slot = bag_owner.reshape(token_count, bag_width).T
    requests, place = pl.pallas_call(
        functools.partial(prep_kernel, piece, shard_rows),
        out_shape=(
            jax.ShapeDtypeStruct((owners, capacity), jnp.int32),
            jax.ShapeDtypeStruct((bag_width, token_count), jnp.int32),
        ),
        in_specs=[vmem, vmem],
        out_specs=(vmem, vmem),
        compiler_params=params,
        name="prep",
    )(rows_by_slot, owner_by_slot)
    received = lax.all_to_all(requests, "table", split_axis=0, concat_axis=0, tiled=True)
    flat_table = tables.reshape(-1, row_width).astype(jnp.float32)
    returned = []
    for number in range(parts):
        sent = pl.pallas_call(
            functools.partial(gather_kernel, number * piece, piece),
            out_shape=jax.ShapeDtypeStruct((owners, piece, row_width), jnp.bfloat16),
            in_specs=[smem, vmem],
            out_specs=vmem,
            scratch_shapes=[pltpu.VMEM((piece, row_width), jnp.float32)],
            compiler_params=params,
            cost_estimate=pl.CostEstimate(
                flops=0, bytes_accessed=24 * 1024 * 1024, transcendentals=0
            ),
            name="owner_gather",
        )(received, flat_table)
        arrived = lax.all_to_all(sent, "table", split_axis=0, concat_axis=0, tiled=True)
        returned.append(arrived.reshape(owners * piece, row_width))
    pooled = pl.pallas_call(
        pool_kernel,
        out_shape=jax.ShapeDtypeStruct((token_count, channels), jnp.bfloat16),
        in_specs=[smem, vmem] + [vmem] * parts,
        out_specs=vmem,
        scratch_shapes=[
            pltpu.VMEM((parts * owners * piece, row_width), jnp.float32),
            pltpu.VMEM((bag_width, token_count, row_width), jnp.float32),
        ],
        compiler_params=params,
        name="pool",
    )(place, bag_weight.reshape(token_count, bag_width), *returned)

    me = lax.axis_index("rep")
    carried = jnp.zeros(stores.shape[1:], stores.dtype)
    for shift in range(copies):
        arrived = stores
        if shift:
            pairs = [(source, (source + shift) % copies) for source in range(copies)]
            arrived = lax.ppermute(stores, "rep", pairs)
        wanted = (returning[0] > 0) & (home[0] == (me + copies - shift) % copies)
        chosen = lax.dynamic_index_in_dim(arrived, entry[0], 0, keepdims=False)
        carried = jnp.where(wanted, chosen, carried)

    hidden = pl.pallas_call(
        conv_kernel,
        out_shape=jax.ShapeDtypeStruct((token_count, channels), jnp.bfloat16),
        in_specs=[vmem] * 4,
        out_specs=vmem,
        scratch_shapes=[
            pltpu.VMEM((token_count + 16, channels), jnp.float32),
            pltpu.VMEM((token_count + 16, channels), jnp.float32),
        ],
        compiler_params=params,
        name="convs",
    )(pooled, carried.astype(jnp.float32), weights, norm_gain)
    return hidden.reshape(samples_here, slot_count, channels)


def solution(mesh):
    in_specs = (
        P(("table", "rep"), None, None),
        P(("table", "rep"), None, None),
        P(("table", "rep"), None, None),
        P(None, "table", None),
        P(("table", "rep")),
        P(("table", "rep")),
        P(("table", "rep")),
        P(("table", "rep"), None, None),
        P(None, "table", None),
        P(),
    )
    out_specs = P(("table", "rep"), None, None)
    return jax.shard_map(local, mesh=mesh, in_specs=in_specs, out_specs=out_specs, check_vma=False)
```

time: 272 us -> 185 us (0.68)
  the two profiles are of different devices: /device:TPU:15 before, /device:TPU:0 now
where the time goes in v1:
time: 185 us; the launch traced here: 183 us
  Pallas kernels  66.8 us (36%)
  waiting for transfers between devices  50.6 us (27%)
  starting transfers between devices  31.2 us (17%)
  between operations  15.5 us (8%)
  local copies, waits for them, and re-layouts  14 us (8%)
  other arithmetic  4.74 us (3%)
    all_to_all x3, waiting for transfers between devices, local(): lax.all_to_all(sent, 'table', split_axis=0, concat_axis=0, tiled=True)  43 us
    pallas_call x3, Pallas kernels, local(): pl.pallas_call(functools.partial(gather_kernel, number * piece, piece), o...  41.6 us
    all_to_all x3, starting transfers between devices, local(): lax.all_to_all(sent, 'table', split_axis=0, concat_axis=0, tiled=True)  22.1 us
    unnamed x23, local copies, waits for them, and re-layouts  13.3 us
    pallas_call x1, Pallas kernels, local(): pl.pallas_call(pool_kernel, out_shape=jax.ShapeDtypeStruct((token_count,...  13.2 us
    pallas_call x1, Pallas kernels, local(): pl.pallas_call(conv_kernel, out_shape=jax.ShapeDtypeStruct((token_count,...  10.8 us
    all_to_all x1, starting transfers between devices, local(): lax.all_to_all(requests, 'table', split_axis=0, concat_axis=0, tiled=True)  7.39 us
    ppermute x1, waiting for transfers between devices, local(): arrived = lax.ppermute(stores, 'rep', pairs)  4.07 us
  transfers between devices with their start and end apart: 6, of which 5 were waited for; matrix products, arithmetic and copies ran while one was open for 4% of the time, Pallas kernels for 31%

profile of v1, /device:TPU:0, one launch (start us, length us, event | category | flops | bytes accessed | tf_op | source)
XLA Modules:
  0.0 182.8 jit_solution(10919806589357112979)
XLA Ops:
  6.5 0.0 all-gather.2.cloned.1.call-start
  6.5 0.7 all-gather.2.cloned.1.call-update
  7.3 0.0 copy-start.6
  7.3 0.7 copy-done.6
  8.0 0.0 copy-start.7
  8.0 0.8 copy-done.7
  8.8 1.2 prep.1
  10.0 0.7 copy.15
  10.7 7.4 %all-to-all-start = ((s32[16,1,768]{2,1,0:T(1,128)}), s32[16,1,768]{2,1,0:T(1,128)S(1)}, u32[]{:S(2)}, u32[]{:S(2)}) async-start(s32[16,1,768]{2,1,0:T(1,128)} %copy.15), calls=%async_computation | async-start | bytes 98304 | tf_op jit(solution)/shard_map/all_to_all | solution.py:166
  18.1 4.0 %bitcast_convert_fusion.table_ref = f32[8192,128]{1,0:T(8,128)} fusion(bf16[4,2048,128]{2,1,0:T(8,128)(2,1)} %param.13), kind=kLoop, calls=%fused_computation | loop fusion | flops 1048576 | bytes 6291456 | tf_op jit(solution)/shard_map/convert_element_type | solution.py:167
  22.0 2.8 %all-to-all-done = s32[16,1,768]{2,1,0:T(1,128)S(1)} async-done(((s32[16,1,768]{2,1,0:T(1,128)}), s32[16,1,768]{2,1,0:T(1,128)S(1)}, u32[]{:S(2)}, u32[]{:S(2)}) %all-to-all-start) | async-done | bytes 49184 | tf_op jit(solution)/shard_map/all_to_all | solution.py:166
  24.8 0.0 copy-start
  24.8 2.2 %copy-done = f32[8192,128]{1,0:T(8,128)S(1)} copy-done((f32[8192,128]{1,0:T(8,128)S(1)}, f32[8192,128]{1,0:T(8,128)}, u32[]{:S(2)}) %copy-start) | copy-done | bytes 4194328
  27.1 13.9 %owner_gather.5 = bf16[16,256,128]{2,1,0:T(8,128)(2,1)} custom-call(s32[16,768]{1,0:T(8,128)S(1)} %bitcast.33, f32[8192,128]{1,0:T(8,128)S(1)} %copy-done), custom_call_target="tpu_custom_call" | custom-call | bytes 25165824 | tf_op jit(solution)/shard_map/owner_gather/pallas_call | solution.py:170
  41.0 3.7 %all-to-all-start.3 = ((bf16[16,256,128]{2,1,0:T(8,128)(2,1)}), bf16[16,256,128]{2,1,0:T(8,128)(2,1)S(1)}, u32[]{:S(2)}, u32[]{:S(2)}) async-start(bf16[16,256,128]{2,1,0:T(8,128)(2,1)} %owner_gather.5), calls=%async_computation.3 | async-start | bytes 2097152 | tf_op jit(solution)/shard_map/all_to_all | solution.py:182
  44.6 0.0 copy-start.1
  44.6 2.2 %copy-done.1 = f32[8192,128]{1,0:T(8,128)S(1)} copy-done((f32[8192,128]{1,0:T(8,128)S(1)}, f32[8192,128]{1,0:T(8,128)}, u32[]{:S(2)}) %copy-start.1) | copy-done | bytes 4194328
  46.8 13.8 %owner_gather.3 = bf16[16,256,128]{2,1,0:T(8,128)(2,1)} custom-call(s32[16,768]{1,0:T(8,128)S(1)} %bitcast.34, f32[8192,128]{1,0:T(8,128)S(1)} %copy-done.1), custom_call_target="tpu_custom_call" | custom-call | bytes 25165824 | tf_op jit(solution)/shard_map/owner_gather/pallas_call | solution.py:170
  60.6 23.9 %all-to-all-done.3 = bf16[16,256,128]{2,1,0:T(8,128)(2,1)S(1)} async-done(((bf16[16,256,128]{2,1,0:T(8,128)(2,1)}), bf16[16,256,128]{2,1,0:T(8,128)(2,1)S(1)}, u32[]{:S(2)}, u32[]{:S(2)}) %all-to-all-start.3) | async-done | bytes 1048608 | tf_op jit(solution)/shard_map/all_to_all | solution.py:182
  84.5 11.5 %all-to-all-start.1 = ((bf16[16,256,128]{2,1,0:T(8,128)(2,1)}), bf16[16,256,128]{2,1,0:T(8,128)(2,1)S(1)}, u32[]{:S(2)}, u32[]{:S(2)}) async-start(bf16[16,256,128]{2,1,0:T(8,128)(2,1)} %owner_gather.3), calls=%async_computation.1 | async-start | bytes 2097152 | tf_op jit(solution)/shard_map/all_to_all | solution.py:182
  96.0 0.0 copy-start.2
  96.0 2.2 %copy-done.2 = f32[8192,128]{1,0:T(8,128)S(1)} copy-done((f32[8192,128]{1,0:T(8,128)S(1)}, f32[8192,128]{1,0:T(8,128)}, u32[]{:S(2)}) %copy-start.2) | copy-done | bytes 4194328
  98.2 0.0 copy-start.9
  98.2 13.9 %owner_gather.4 = bf16[16,256,128]{2,1,0:T(8,128)(2,1)} custom-call(s32[16,768]{1,0:T(8,128)S(1)} %bitcast.35, f32[8192,128]{1,0:T(8,128)S(1)} %copy-done.2), custom_call_target="tpu_custom_call" | custom-call | bytes 25165824 | tf_op jit(solution)/shard_map/owner_gather/pallas_call | solution.py:170
  112.1 0.0 copy-start.8
  112.1 6.8 %all-to-all-done.1 = bf16[16,256,128]{2,1,0:T(8,128)(2,1)S(1)} async-done(((bf16[16,256,128]{2,1,0:T(8,128)(2,1)}), bf16[16,256,128]{2,1,0:T(8,128)(2,1)S(1)}, u32[]{:S(2)}, u32[]{:S(2)}) %all-to-all-start.1) | async-done | bytes 1048608 | tf_op jit(solution)/shard_map/all_to_all | solution.py:182
  118.9 6.9 %all-to-all-start.2 = ((bf16[16,256,128]{2,1,0:T(8,128)(2,1)}), bf16[16,256,128]{2,1,0:T(8,128)(2,1)S(1)}, u32[]{:S(2)}, u32[]{:S(2)}) async-start(bf16[16,256,128]{2,1,0:T(8,128)(2,1)} %owner_gather.4), calls=%async_computation.2 | async-start | bytes 2097152 | tf_op jit(solution)/shard_map/all_to_all | solution.py:182
  125.8 1.0 copy.16
  126.8 1.8 collective-permute-start
  130.6 0.0 copy-done.9
  130.6 1.0 copy.14
  131.6 4.1 %collective-permute-done = bf16[8,30,512]{2,1,0:T(8,128)(2,1)} collective-permute-done((bf16[8,30,512]{2,1,0:T(8,128)(2,1)S(1)}, bf16[8,30,512]{2,1,0:T(8,128)(2,1)}, u32[]{:S(2)}, u32[]{:S(2)}) %collective-permute-start) | collective-permute-done | bytes 245792 | tf_op jit(solution)/shard_map/ppermute | solution.py:203
  135.7 0.8 bitcast_convert_fusion.1.carried_ref
  136.4 12.3 %all-to-all-done.2 = bf16[16,256,128]{2,1,0:T(8,128)(2,1)S(1)} async-done(((bf16[16,256,128]{2,1,0:T(8,128)(2,1)}), bf16[16,256,128]{2,1,0:T(8,128)(2,1)S(1)}, u32[]{:S(2)}, u32[]{:S(2)}) %all-to-all-start.2) | async-done | bytes 1048608 | tf_op jit(solution)/shard_map/all_to_all | solution.py:182
  148.8 0.0 copy-start.3
  148.8 1.0 copy-done.3
  149.7 0.0 copy-start.4
  149.7 1.2 copy-done.4
  151.0 0.0 copy-start.5
  151.0 1.0 copy-done.5
  152.0 13.2 %pool.1.pooled_ref = bf16[1024,512]{1,0:T(8,128)(2,1)S(1)} custom-call(s32[8,1024]{1,0:T(8,128)S(1)} %get-tuple-element.7.place_ref, f32[1024,8]{1,0:T(8,128)S(1)} %bitcast.32, bf16[4096,128]{1,0:T(8,128)(2,1)S(1)} %bitcast.30, bf16[4096,128]{1,0:T(8,128)(2,1)S(1)} %bitcast.31, bf16[4096,128]{1,0:T(8,128)(2,1)S(1)} %bitcast.29), custom_call_target="tpu_custom_call" | custom-call | tf_op jit(solution)/shard_map/pool/pallas_call | solution.py:184
  165.2 0.0 all-gather.2.cloned.1.call-done.weight_ref
  165.2 0.0 copy-done.8
  165.2 10.8 %convs.1 = bf16[1024,512]{1,0:T(8,128)(2,1)} custom-call(bf16[1024,512]{1,0:T(8,128)(2,1)S(1)} %pool.1.pooled_ref, f32[30,512]{1,0:T(8,128)S(1)} %bitcast_convert_fusion.1.carried_ref, bf16[4,1536,512]{2,1,0:T(8,128)(2,1)} %all-gather.2.cloned.1.call-done.weight_ref, f32[4,512]{1,0:T(4,128)S(1)} %copy-done.8), custom_call_target="tpu_custom_call" | custom-call | tf_op jit(solution)/shard_map/convs/pallas_call | solution.py:208
  (1 shorter events, 0.0 us)
Async XLA Ops:
  6.5 158.7 %all-gather.2.cloned.1.call-start = ((), (), s32[]{:S(2)}) async-start(), calls=%async_computation.4 | async-start | bytes 6684672 | tf_op jit(solution)/shard_map/all_gather | solution.py:151
  7.3 0.8 copy-start.6
  8.0 0.8 copy-start.7
  10.7 14.2 %all-to-all-start = ((s32[16,1,768]{2,1,0:T(1,128)}), s32[16,1,768]{2,1,0:T(1,128)S(1)}, u32[]{:S(2)}, u32[]{:S(2)}) async-start(s32[16,1,768]{2,1,0:T(1,128)} %copy.15), calls=%async_computation | async-start | bytes 98304 | tf_op jit(solution)/shard_map/all_to_all | solution.py:166
  24.8 2.2 %copy-start = (f32[8192,128]{1,0:T(8,128)S(1)}, f32[8192,128]{1,0:T(8,128)}, u32[]{:S(2)}) copy-start(f32[8192,128]{1,0:T(8,128)} %bitcast_convert_fusion.table_ref) | copy-start | bytes 12582916
  41.0 43.5 %all-to-all-start.3 = ((bf16[16,256,128]{2,1,0:T(8,128)(2,1)}), bf16[16,256,128]{2,1,0:T(8,128)(2,1)S(1)}, u32[]{:S(2)}, u32[]{:S(2)}) async-start(bf16[16,256,128]{2,1,0:T(8,128)(2,1)} %owner_gather.5), calls=%async_computation.3 | async-start | bytes 2097152 | tf_op jit(solution)/shard_map/all_to_all | solution.py:182
  44.6 2.2 %copy-start.1 = (f32[8192,128]{1,0:T(8,128)S(1)}, f32[8192,128]{1,0:T(8,128)}, u32[]{:S(2)}) copy-start(f32[8192,128]{1,0:T(8,128)} %bitcast_convert_fusion.table_ref) | copy-start | bytes 12582916
  84.5 34.5 %all-to-all-start.1 = ((bf16[16,256,128]{2,1,0:T(8,128)(2,1)}), bf16[16,256,128]{2,1,0:T(8,128)(2,1)S(1)}, u32[]{:S(2)}, u32[]{:S(2)}) async-start(bf16[16,256,128]{2,1,0:T(8,128)(2,1)} %owner_gather.3), calls=%async_computation.1 | async-start | bytes 2097152 | tf_op jit(solution)/shard_map/all_to_all | solution.py:182
  96.0 2.2 %copy-start.2 = (f32[8192,128]{1,0:T(8,128)S(1)}, f32[8192,128]{1,0:T(8,128)}, u32[]{:S(2)}) copy-start(f32[8192,128]{1,0:T(8,128)} %bitcast_convert_fusion.table_ref) | copy-start | bytes 12582916
  98.2 32.4 %copy-start.9 = (f32[1,1024,8]{1,2,0:T(8,128)S(1)}, f32[1,1024,8]{1,2,0:T(8,128)}, u32[]{:S(2)}) copy-start(f32[1,1024,8]{1,2,0:T(8,128)} %param.12) | copy-start | bytes 98308
  112.1 53.1 %copy-start.8 = (f32[4,512]{1,0:T(4,128)S(1)}, f32[4,512]{1,0:T(4,128)}, u32[]{:S(2)}) copy-start(f32[4,512]{1,0:T(4,128)} %gain_ref.1) | copy-start | bytes 24580
  118.9 29.8 %all-to-all-start.2 = ((bf16[16,256,128]{2,1,0:T(8,128)(2,1)}), bf16[16,256,128]{2,1,0:T(8,128)(2,1)S(1)}, u32[]{:S(2)}, u32[]{:S(2)}) async-start(bf16[16,256,128]{2,1,0:T(8,128)(2,1)} %owner_gather.4), calls=%async_computation.2 | async-start | bytes 2097152 | tf_op jit(solution)/shard_map/all_to_all | solution.py:182
  126.8 8.8 %collective-permute-start = (bf16[8,30,512]{2,1,0:T(8,128)(2,1)S(1)}, bf16[8,30,512]{2,1,0:T(8,128)(2,1)}, u32[]{:S(2)}, u32[]{:S(2)}) collective-permute-start(bf16[8,30,512]{2,1,0:T(8,128)(2,1)S(1)} %copy.16), channel_id=1, source_target_pairs={{0,1},{1,0},{2,3},{3,2},{4,5},{5,4},{6,7},{7,6},{8,9},{9,8},{10,11... | collective-permute-start | bytes 737288 | tf_op jit(solution)/shard_map/ppermute | solution.py:203
  148.8 1.0 copy-start.3
  149.7 1.2 copy-start.4
  151.0 1.0 copy-start.5
Sparse Core Ops, SparseCore 0:
  9.6 84.4 all-gather.1

commit v2 on v1

v2 whole, which is shorter than its diff:
```python
import functools
import jax
import jax.numpy as jnp
from jax import lax
from jax.experimental import pallas as pl
from jax.experimental.pallas import tpu as pltpu
from jax.sharding import PartitionSpec as P

table_of_id = (0, 1, 2, 2, 3, 3, 3, 3)
bag_bounds = ((0, 1), (1, 2), (2, 4), (4, 8))
epsilon = 1e-05
parts = 3
unroll = 16
megabyte = 1024 * 1024


def prep_kernel(cuts, shard_rows, rows_ref, owner_ref, request_ref, place_ref):
    owner = owner_ref[...]
    rows = rows_ref[...]
    owners = request_ref.shape[0]
    width, slots = owner.shape
    value_bits = (len(bag_bounds) * shard_rows).bit_length()
    owner_ids = lax.broadcasted_iota(jnp.int32, (owners, slots), 0)
    lane = lax.broadcasted_iota(jnp.int32, (owners, slots), 1)
    value = jnp.zeros((owners, slots), jnp.int32)
    for k in range(width):
        named = owner[k : k + 1, :] == owner_ids
        value = jnp.where(named, rows[k : k + 1, :] + (table_of_id[k] * shard_rows + 1), value)
    present = jnp.where(value > 0, 1, 0)
    rank = present
    step = 1
    while step < slots:
        rank = rank + jnp.where(lane >= step, pltpu.roll(rank, step, 1), 0)
        step *= 2
    rank = rank - present
    place = jnp.zeros((width, slots), jnp.int32)
    for number in range(owners):
        place = jnp.where(owner == number, rank[number : number + 1, :], place)
    landing = jnp.zeros((width, slots), jnp.int32)
    for start, stop in zip(cuts[:-1], cuts[1:]):
        where = owners * start + owner * (stop - start) + place - start
        landing = jnp.where(place >= start, where, landing)
    place_ref[...] = landing
    packed = jnp.where(value > 0, ((lane - rank) << value_bits) + value, 0)
    step = 1
    level = value_bits
    while step < slots:
        moving = jnp.where(((packed >> level) & 1) == 1, packed, 0)
        packed = (packed - moving) + pltpu.roll(moving, slots - step, 1)
        step *= 2
        level += 1
    value = jnp.maximum((packed & ((1 << value_bits) - 1)) - 1, 0)
    request_ref[...] = value[:, : request_ref.shape[1]]


def gather_kernel(capacity, first, index_ref, table_ref, out_ref, scratch):
    owners, piece, _ = out_ref.shape

    def one_owner(number, carry):
        origin = number * capacity + first

        def some_rows(block, inner):
            base = pl.multiple_of(block * unroll, unroll)
            picks = [index_ref[origin + base + i] for i in range(unroll)]
            rows = [table_ref[pick] for pick in picks]
            for i in range(unroll):
                scratch[pl.ds(base + i, 1), :] = rows[i]
            return inner

        lax.fori_loop(0, piece // unroll, some_rows, 0)
        out_ref[number] = scratch[...].astype(jnp.bfloat16)
        return carry

    lax.fori_loop(0, owners, one_owner, 0)


def stage_kernel(number, first, place_ref, weight_ref, carried_ref, filter_ref, gain_ref, *refs):
    piece_refs = refs[: number + 1]
    refs = refs[number + 1 + (number > 0) :]
    out_ref, state_ref, table, picked, first_buf, second_buf, result, semaphore = refs
    width, slots, lanes = picked.shape
    start = 0
    for piece_ref in piece_refs:
        count = piece_ref.shape[0]
        rows = 256

        def widen(step, carry, piece_ref=piece_ref, start=start):
            base = pl.multiple_of(step * rows, rows)
            table[pl.ds(start + base, rows), :] = piece_ref[pl.ds(base, rows), :].astype(jnp.float32)
            return carry

        lax.fori_loop(0, count // rows, widen, 0)
        start += count

    def some_slots(step, carry):
        base = pl.multiple_of(step * 8, 8)
        for k in range(width):
            picks = [place_ref[k, first + base + i] for i in range(8)]
            rows = [table[pl.ds(pick, 1), :] for pick in picks]
            for i in range(8):
                picked[k, pl.ds(base + i, 1), :] = rows[i]
        return carry

    lax.fori_loop(0, slots // 8, some_slots, 0)
    front = 16
    for t, (lower, upper) in enumerate(bag_bounds):
        total = picked[lower] * weight_ref[first : first + slots, lower : lower + 1]
        for k in range(lower + 1, upper):
            total = total + picked[k] * weight_ref[first : first + slots, k : k + 1]
        total = total.astype(jnp.bfloat16).astype(jnp.float32)
        first_buf[front:, t * lanes : (t + 1) * lanes] = total

    layers = filter_ref.shape[0]
    offset = 0
    for layer in range(layers):
        dilation = 2**layer
        span = 2 * dilation
        source, target = (first_buf, second_buf) if layer % 2 == 0 else (second_buf, first_buf)
        source[front - span : front, :] = carried_ref[offset : offset + span, :]
        state_ref[offset : offset + span, :] = source[front + slots - span : front + slots, :]
        offset += span
        for begin in range(0, slots, 256):
            rows = min(256, slots - begin)
            base = front + begin
            taps = [
                source[base - tap * dilation : base - tap * dilation + rows, :].astype(jnp.bfloat16)
                for tap in range(3)
            ]
            output = jnp.dot(
                jnp.concatenate(taps, axis=1), filter_ref[layer], preferred_element_type=jnp.float32
            )
            mean = jnp.mean(output, axis=-1, keepdims=True)
            centred = output - mean
            spread = jnp.mean(centred * centred, axis=-1, keepdims=True)
            active = jnp.maximum(
                centred * lax.rsqrt(spread + epsilon) * gain_ref[layer : layer + 1, :], 0.0
            )
            if layer % 2 == 1:
                active = active + target[base : base + rows, :]
            active = active.astype(jnp.bfloat16)
            if layer == layers - 1:
                result[begin : begin + rows, :] = active
            else:
                target[base : base + rows, :] = active.astype(jnp.float32)
    copy = pltpu.make_async_copy(result, out_ref.at[pl.ds(first, slots), :], semaphore)
    copy.start()
    copy.wait()


def gather_filters(conv_weight):
    owners = lax.axis_size("table")
    copies = lax.axis_size("rep")
    layers, depth, channels = conv_weight.shape
    if owners % 2 or copies % 2 or layers % 2:
        return lax.all_gather(conv_weight, "table", axis=1, tiled=True)
    half = layers // 2
    parity = lax.axis_index("table") % 2
    side = lax.axis_index("rep") % 2
    groups = [list(range(start, owners, 2)) for start in range(2)]
    mine = lax.dynamic_slice_in_dim(conv_weight, side * half, half, 0)
    mine = lax.all_gather(mine, "table", axis_index_groups=groups, axis=0, tiled=False)
    other = lax.ppermute(mine, "rep", [(r, r ^ 1) for r in range(copies)])
    low = jnp.where(side == 0, mine, other)
    high = jnp.where(side == 0, other, mine)
    own = jnp.concatenate([low, high], axis=1)
    partner = lax.ppermute(own, "table", [(i, i ^ 1) for i in range(owners)])
    even = jnp.where(parity == 0, own, partner)
    odd = jnp.where(parity == 0, partner, own)
    both = jnp.stack([even, odd], axis=1)
    return jnp.transpose(both, (2, 0, 1, 3, 4)).reshape(layers, owners * depth, channels)


def local(
    bag_rows, bag_owner, bag_weight, tables, returning, home, entry, stores, conv_weight, norm_gain
):
    owners = lax.axis_size("table")
    copies = lax.axis_size("rep")
    samples_here, slot_count, bag_width = bag_rows.shape
    token_count = samples_here * slot_count
    shard_rows = tables.shape[1]
    row_width = tables.shape[2]
    channels = conv_weight.shape[-1]
    capacity = min(token_count, (3 * token_count * bag_width + 2 * owners - 1) // (2 * owners))
    cuts = [capacity * cut // parts for cut in range(parts + 1)]
    slot_cuts = cuts[:-1] + [token_count]
    smem = pl.BlockSpec(memory_space=pltpu.SMEM)
    vmem = pl.BlockSpec(memory_space=pltpu.VMEM)
    anywhere = pl.BlockSpec(memory_space=pl.ANY)

    filters = gather_filters(conv_weight)

    rows_by_slot = bag_rows.reshape(token_count, bag_width).T
    owner_by_slot = bag_owner.reshape(token_count, bag_width).T
    requests, place = pl.pallas_call(
        functools.partial(prep_kernel, cuts, shard_rows),
        out_shape=(
            jax.ShapeDtypeStruct((owners, capacity), jnp.int32),
            jax.ShapeDtypeStruct((bag_width, token_count), jnp.int32),
        ),
        in_specs=[vmem, vmem],
        out_specs=(vmem, vmem),
        compiler_params=pltpu.CompilerParams(vmem_limit_bytes=8 * megabyte),
        name="prep",
    )(rows_by_slot, owner_by_slot)
    received = lax.all_to_all(requests, "table", split_axis=0, concat_axis=0, tiled=True)
    received = received.reshape(owners * capacity)
    wide_table = tables.astype(jnp.float32).reshape(-1, 1, row_width)
    returned = []
    for number in range(parts):
        piece = cuts[number + 1] - cuts[number]
        sent = pl.pallas_call(
            functools.partial(gather_kernel, capacity, cuts[number]),
            out_shape=jax.ShapeDtypeStruct((owners, piece, row_width), jnp.bfloat16),
            in_specs=[smem, vmem],
            out_specs=vmem,
            scratch_shapes=[pltpu.VMEM((piece, row_width), jnp.float32)],
            compiler_params=pltpu.CompilerParams(vmem_limit_bytes=12 * megabyte),
            cost_estimate=pl.CostEstimate(
                flops=0, bytes_accessed=20 * megabyte, transcendentals=0
            ),
            name="owner_gather",
        )(received, wide_table)
        arrived = lax.all_to_all(sent, "table", split_axis=0, concat_axis=0, tiled=True)
        returned.append(arrived.reshape(owners * piece, row_width))

    me = lax.axis_index("rep")
    carried = jnp.zeros(stores.shape[1:], stores.dtype)
    for shift in range(copies):
        arrived = stores
        if shift:
            pairs = [(source, (source + shift) % copies) for source in range(copies)]
            arrived = lax.ppermute(stores, "rep", pairs)
        wanted = (returning[0] > 0) & (home[0] == (me + copies - shift) % copies)
        chosen = lax.dynamic_index_in_dim(arrived, entry[0], 0, keepdims=False)
        carried = jnp.where(wanted, chosen, carried)

    state = carried.astype(jnp.float32)
    weight_by_slot = bag_weight.reshape(token_count, bag_width)
    hidden = None
    for number in range(parts):
        first, last = slot_cuts[number], slot_cuts[number + 1]
        slots = last - first
        known = [] if hidden is None else [hidden]
        hidden, state = pl.pallas_call(
            functools.partial(stage_kernel, number, first),
            out_shape=(
                jax.ShapeDtypeStruct((token_count, channels), jnp.bfloat16),
                jax.ShapeDtypeStruct(state.shape, jnp.float32),
            ),
            in_specs=[smem] + [vmem] * (5 + number) + [anywhere] * len(known),
            out_specs=(anywhere, vmem),
            scratch_shapes=[
                pltpu.VMEM((owners * cuts[number + 1], row_width), jnp.float32),
                pltpu.VMEM((bag_width, slots, row_width), jnp.float32),
                pltpu.VMEM((slots + 16, channels), jnp.float32),
                pltpu.VMEM((slots + 16, channels), jnp.float32),
                pltpu.VMEM((slots, channels), jnp.bfloat16),
                pltpu.SemaphoreType.DMA,
            ],
            input_output_aliases={6 + number: 0} if known else {},
            compiler_params=pltpu.CompilerParams(vmem_limit_bytes=32 * megabyte),
            cost_estimate=pl.CostEstimate(
                flops=2 * slots * 3 * channels * channels * conv_weight.shape[0],
                bytes_accessed=24 * megabyte,
                transcendentals=0,
            ),
            name="stage",
        )(place, weight_by_slot, state, filters, norm_gain, *returned[: number + 1], *known)
    return hidden.reshape(samples_here, slot_count, channels)


def solution(mesh):
    in_specs = (
        P(("table", "rep"), None, None),
        P(("table", "rep"), None, None),
        P(("table", "rep"), None, None),
        P(None, "table", None),
        P(("table", "rep")),
        P(("table", "rep")),
        P(("table", "rep")),
        P(("table", "rep"), None, None),
        P(None, "table", None),
        P(),
    )
    out_specs = P(("table", "rep"), None, None)
    return jax.shard_map(local, mesh=mesh, in_specs=in_specs, out_specs=out_specs, check_vma=False)
```

time: 185 us -> 198 us (1.070)
  waiting for transfers between devices: 50.6 us -> 80.3 us
  Pallas kernels: 66.8 us -> 50.9 us
  starting transfers between devices: 31.2 us -> 23 us
  other arithmetic: 4.74 us -> 12.3 us
    all_gather x1, waiting for transfers between devices: 0.02 us -> 48.2 us  [gather_filters(): lax.all_gather(mine, 'table', axis_index_groups=groups, axis=0, tiled=False)]
    all_to_all x3, waiting for transfers between devices: 43 us -> 13.8 us  [local(): lax.all_to_all(sent, 'table', split_axis=0, concat_axis=0, tiled=True)]
    pallas_call x6 -> x7, Pallas kernels: 66.8 us -> 50.9 us  [the longest x3 28.9 us: local(): pl.pallas_call(functools.partial(stage_kernel, number, first), out_shape=...]
    ppermute x0 -> x2, waiting for transfers between devices: none -> 9.4 us  [the longest x1 9.4 us: gather_filters(): other = lax.ppermute(mine, 'rep', [(r, r ^ 1) for r in range(copies)])]
    all_to_all x3, starting transfers between devices: 22.1 us -> 17.4 us  [local(): lax.all_to_all(sent, 'table', split_axis=0, concat_axis=0, tiled=True)]
    convert_element_type x2 -> x1, other arithmetic: 4.74 us -> 0.77 us  [local(): state = carried.astype(jnp.float32)]
    all_to_all x1, starting transfers between devices: 7.39 us -> 3.52 us  [local(): lax.all_to_all(requests, 'table', split_axis=0, concat_axis=0, tiled=True)]
    reshape x0 -> x1, other arithmetic: none -> 3.83 us  [local(): wide_table = tables.astype(jnp.float32).reshape(-1, 1, row_width)]
  transfers between devices with their start and end apart: 6 -> 8, of which waited for: 5 -> 5; matrix products, arithmetic and copies ran while one was open for 4% -> 7% of each run, Pallas kernels for 31% -> 19%
where the time goes in v2:
time: 198 us; the launch traced here: 197 us
  waiting for transfers between devices  80.3 us (41%)
  Pallas kernels  50.9 us (26%)
  starting transfers between devices  23 us (12%)
  between operations  15.6 us (8%)
  local copies, waits for them, and re-layouts  15.1 us (8%)
  other arithmetic  12.3 us (6%)
    all_gather x1, waiting for transfers between devices, gather_filters(): lax.all_gather(mine, 'table', axis_index_groups=groups, axis=0, tiled=False)  48.2 us
    pallas_call x3, Pallas kernels, local(): pl.pallas_call(functools.partial(stage_kernel, number, first), out_shape=...  28.9 us
    pallas_call x3, Pallas kernels, local(): pl.pallas_call(functools.partial(gather_kernel, capacity, cuts[number]),...  20.8 us
    all_to_all x3, starting transfers between devices, local(): lax.all_to_all(sent, 'table', split_axis=0, concat_axis=0, tiled=True)  17.4 us
    all_to_all x3, waiting for transfers between devices, local(): lax.all_to_all(sent, 'table', split_axis=0, concat_axis=0, tiled=True)  13.8 us
    unnamed x28, local copies, waits for them, and re-layouts  10.9 us
    ppermute x1, waiting for transfers between devices, gather_filters(): other = lax.ppermute(mine, 'rep', [(r, r ^ 1) for r in range(copies)])  9.4 us
    ppermute x1, waiting for transfers between devices, local(): arrived = lax.ppermute(stores, 'rep', pairs)  5.92 us
  transfers between devices with their start and end apart: 8, of which 5 were waited for; matrix products, arithmetic and copies ran while one was open for 7% of the time, Pallas kernels for 19%

profile of v2, /device:TPU:0, one launch (start us, length us, event | category | flops | bytes accessed | tf_op | source)
XLA Modules:
  0.0 197.2 jit_solution(10234908924504843916)
XLA Ops:
  6.5 0.0 copy-start
  6.5 0.0 all-gather.3.cloned.1.call-start
  6.6 1.0 copy-done
  7.5 0.7 constant_dynamic-slice_fusion
  8.2 0.0 all-gather.3.cloned.1.call-update
  8.2 48.2 %all-gather.3.cloned.1.call-done = bf16[16,96,512]{2,1,0:T(8,128)(2,1)} async-done(((bf16[2,96,512]{2,1,0:T(8,128)(2,1)}), bf16[16,96,512]{2,1,0:T(8,128)(2,1)}) %all-gather.3.cloned.1.call-update) | async-done | bytes 1572880 | tf_op jit(solution)/shard_map/all_gather | solution.py:161
  56.5 2.8 %copy.24 = bf16[8,2,96,512]{3,2,0,1:T(8,128)(2,1)} copy(bf16[8,2,96,512]{3,2,1,0:T(8,128)(2,1)} %bitcast.55) | data formatting | bytes 3145728 | tf_op jit(solution)/shard_map/all_gather | solution.py:161
  59.2 1.5 collective-permute-start.1
  60.7 0.0 copy-done.7
  60.7 0.0 copy-done.6
  60.7 1.2 prep.1
  61.9 0.7 copy.27
  62.6 3.5 %all-to-all-start = ((s32[16,1,768]{2,1,0:T(1,128)}), s32[16,1,768]{2,1,0:T(1,128)S(1)}, u32[]{:S(2)}, u32[]{:S(2)}) async-start(s32[16,1,768]{2,1,0:T(1,128)} %copy.27), calls=%async_computation | async-start | bytes 98304 | tf_op jit(solution)/shard_map/all_to_all | solution.py:205
  66.1 3.8 %reshape.56 = f32[4,2048,128]{2,1,0:T(8,128)} convert(bf16[4,2048,128]{2,1,0:T(8,128)(2,1)} %param.13) | non-fusion elementwise | flops 1048576 | bytes 6291456 | tf_op jit(solution)/shard_map/reshape | solution.py:207
  70.0 2.9 %all-to-all-done = s32[16,1,768]{2,1,0:T(1,128)S(1)} async-done(((s32[16,1,768]{2,1,0:T(1,128)}), s32[16,1,768]{2,1,0:T(1,128)S(1)}, u32[]{:S(2)}, u32[]{:S(2)}) %all-to-all-start) | async-done | bytes 49184 | tf_op jit(solution)/shard_map/all_to_all | solution.py:205
  72.9 2.2 %copy-done.1 = f32[4,2048,128]{2,1,0:T(8,128)S(1)} copy-done((f32[4,2048,128]{2,1,0:T(8,128)S(1)}, f32[4,2048,128]{2,1,0:T(8,128)}, u32[]{:S(2)}) %copy-start.1) | copy-done | bytes 4194328
  75.1 6.9 %owner_gather.3 = bf16[16,256,128]{2,1,0:T(8,128)(2,1)} custom-call(s32[12288]{0:T(1024)S(1)} %bitcast.49, f32[8192,1,128]{2,1,0:T(1,128)S(1)} %bitcast.35), custom_call_target="tpu_custom_call" | custom-call | bytes 20971520 | tf_op jit(solution)/shard_map/owner_gather/pallas_call | solution.py:211
  82.0 3.7 %all-to-all-start.1 = ((bf16[16,256,128]{2,1,0:T(8,128)(2,1)}), bf16[16,256,128]{2,1,0:T(8,128)(2,1)S(1)}, u32[]{:S(2)}, u32[]{:S(2)}) async-start(bf16[16,256,128]{2,1,0:T(8,128)(2,1)} %owner_gather.3), calls=%async_computation.1 | async-start | bytes 2097152 | tf_op jit(solution)/shard_map/all_to_all | solution.py:223
  85.7 9.4 %collective-permute-done.1 = bf16[8,2,96,512]{3,2,0,1:T(8,128)(2,1)} collective-permute-done((bf16[8,2,96,512]{3,2,0,1:T(8,128)(2,1)}, bf16[8,2,96,512]{3,2,0,1:T(8,128)(2,1)}, u32[]{:S(2)}, u32[]{:S(2)}) %collective-permute-start.1) | collective-permute-done | bytes 1572896 | tf_op jit(solution)/shard_map/ppermute | solution.py:162
  95.1 2.1 %broadcast_select_fusion.1 = (bf16[8,2,96,512]{3,2,0,1:T(8,128)(2,1)S(1)}, bf16[8,2,96,512]{3,2,0,1:T(8,128)(2,1)S(1)}) fusion(bf16[8,2,96,512]{3,2,0,1:T(8,128)(2,1)} %collective-permute-done.1, pred[]{:T(512)S(6)} %eq.22, bf16[8,2,96,512]{3,2,1,0:T(8,128)(2,1)} %bitcast.56), kind=kLoop, calls=%fused_computation.5 | loop fusion | flops 1572864 | bytes 6291457 | tf_op jit(solution)/shard_map/jit(_where)/select_n | solution.py:163
  97.2 2.0 %pad_maximum_fusion.1 = bf16[8,4,96,512]{3,2,0,1:T(8,128)(2,1)} fusion(bf16[8,2,96,512]{3,2,0,1:T(8,128)(2,1)S(1)} %get-tuple-element.22, bf16[8,2,96,512]{3,2,0,1:T(8,128)(2,1)S(1)} %get-tuple-element.21), kind=kLoop, calls=%fused_computation.1 | loop fusion | flops 1572864 | bytes 6291456 | tf_op jit(solution)/shard_map/concatenate | solution.py:165
  99.2 0.4 copy-done.9
  99.6 0.8 copy-done.10
  100.4 0.0 collective-permute-start.2
  100.4 1.3 copy-done.2
  101.6 6.9 %owner_gather.4 = bf16[16,256,128]{2,1,0:T(8,128)(2,1)} custom-call(s32[12288]{0:T(1024)S(1)} %bitcast.50, f32[8192,1,128]{2,1,0:T(1,128)S(1)} %bitcast.36), custom_call_target="tpu_custom_call" | custom-call | bytes 20971520 | tf_op jit(solution)/shard_map/owner_gather/pallas_call | solution.py:211
  108.6 0.0 all-to-all-done.1
  108.6 6.8 %all-to-all-start.2 = ((bf16[16,256,128]{2,1,0:T(8,128)(2,1)}), bf16[16,256,128]{2,1,0:T(8,128)(2,1)S(1)}, u32[]{:S(2)}, u32[]{:S(2)}) async-start(bf16[16,256,128]{2,1,0:T(8,128)(2,1)} %owner_gather.4), calls=%async_computation.2 | async-start | bytes 2097152 | tf_op jit(solution)/shard_map/all_to_all | solution.py:223
  115.4 2.2 %copy-done.3 = f32[4,2048,128]{2,1,0:T(8,128)S(1)} copy-done((f32[4,2048,128]{2,1,0:T(8,128)S(1)}, f32[4,2048,128]{2,1,0:T(8,128)}, u32[]{:S(2)}) %copy-start.3) | copy-done | bytes 4194328
  117.6 7.0 %owner_gather.5 = bf16[16,256,128]{2,1,0:T(8,128)(2,1)} custom-call(s32[12288]{0:T(1024)S(1)} %bitcast.51, f32[8192,1,128]{2,1,0:T(1,128)S(1)} %bitcast.37), custom_call_target="tpu_custom_call" | custom-call | bytes 20971520 | tf_op jit(solution)/shard_map/owner_gather/pallas_call | solution.py:211
  124.5 13.8 %all-to-all-done.2 = bf16[16,256,128]{2,1,0:T(8,128)(2,1)S(1)} async-done(((bf16[16,256,128]{2,1,0:T(8,128)(2,1)}), bf16[16,256,128]{2,1,0:T(8,128)(2,1)S(1)}, u32[]{:S(2)}, u32[]{:S(2)}) %all-to-all-start.2) | async-done | bytes 1048608 | tf_op jit(solution)/shard_map/all_to_all | solution.py:223
  138.3 6.9 %all-to-all-start.3 = ((bf16[16,256,128]{2,1,0:T(8,128)(2,1)}), bf16[16,256,128]{2,1,0:T(8,128)(2,1)}, u32[]{:S(2)}, u32[]{:S(2)}) async-start(bf16[16,256,128]{2,1,0:T(8,128)(2,1)} %owner_gather.5), calls=%async_computation.3 | async-start | bytes 2097152 | tf_op jit(solution)/shard_map/all_to_all | solution.py:223
  145.3 0.0 copy-done.11
  145.3 0.1 copy.21
  145.4 0.6 collective-permute-start
  148.0 0.2 copy.20
  148.2 5.9 %collective-permute-done = bf16[8,30,512]{2,1,0:T(8,128)(2,1)} collective-permute-done((bf16[8,30,512]{2,1,0:T(8,128)(2,1)S(1)}, bf16[8,30,512]{2,1,0:T(8,128)(2,1)}, u32[]{:S(2)}, u32[]{:S(2)}) %collective-permute-start) | collective-permute-done | bytes 245792 | tf_op jit(solution)/shard_map/ppermute | solution.py:232
  154.1 0.8 bitcast_convert_fusion.carried_ref
  154.9 0.0 collective-permute-done.2
  154.9 3.0 %select_bitcast_fusion.1 = (bf16[8,1,4,96,512]{4,3,1,0,2:T(8,128)(2,1)S(1)}, bf16[8,1,4,96,512]{4,3,1,0,2:T(8,128)(2,1)S(1)}) fusion(bf16[8,4,96,512]{3,2,0,1:T(8,128)(2,1)} %collective-permute-done.2, pred[]{:T(512)S(6)} %eq.21, bf16[8,2,96,512]{3,2,0,1:T(8,128)(2,1)} %copy-done.10, bf16[8,2,96,512]{3,2,0,1:T(8,128)(2,1)} %copy-done.9), kind=kLoop, calls=%fused_computation.3 | loop fusion | flops 4718592 | bytes 12582913 | tf_op jit(solution)/shard_map/stack | solution.py:169
  157.9 0.0 copy-start.8
  157.9 0.6 pad_maximum_fusion
  158.5 0.1 copy-done.8
  158.6 7.9 %stage.3 = (bf16[1024,512]{1,0:T(8,128)(2,1)}, f32[30,512]{1,0:T(8,128)S(1)}) custom-call(s32[8,1024]{1,0:T(8,128)S(1)} %get-tuple-element.12.place_ref, f32[1024,8]{1,0:T(8,128)S(1)} %bitcast.44, f32[30,512]{1,0:T(8,128)S(1)} %bitcast_convert_fusion.carried_ref, bf16[4,1536,512]{2,1,0:T(8,128)(2,1)S(1)} %bitcast.38, f32[4,512]{1,0:T(4,128)S(1)} %copy-done.8, ...), custom_call_target="tpu_custom_call" | custom-call | flops 1610612736 | bytes 25165824 | tf_op jit(solution)/shard_map/stage/pallas_call | solution.py:244
  166.6 8.2 %stage.4 = (bf16[1024,512]{1,0:T(8,128)(2,1)}, f32[30,512]{1,0:T(8,128)S(1)}) custom-call(s32[8,1024]{1,0:T(8,128)S(1)} %get-tuple-element.12.place_ref, f32[1024,8]{1,0:T(8,128)S(1)} %bitcast.45, f32[30,512]{1,0:T(8,128)S(1)} %get-tuple-element.14.carried_ref, bf16[4,1536,512]{2,1,0:T(8,128)(2,1)S(1)} %bitcast.39, ...), custom_call_target="tpu_custom_call", output_to_operand_aliasing={{0}: (7, {})} | custom-call | flops 1610612736 | bytes 25165824 | tf_op jit(solution)/shard_map/stage/pallas_call | solution.py:244
  174.8 0.0 all-to-all-done.3
  174.8 2.8 %copy-done.5 = bf16[8,2,4,96,512]{4,3,1,0,2:T(8,128)(2,1)S(1)} copy-done((bf16[8,2,4,96,512]{4,3,1,0,2:T(8,128)(2,1)S(1)}, bf16[8,2,4,96,512]{4,3,1,0,2:T(8,128)(2,1)}, u32[]{:S(2)}) %copy-start.5) | copy-done | bytes 6291480
  177.6 12.7 %stage.5 = (bf16[1024,512]{1,0:T(8,128)(2,1)}, f32[30,512]{1,0:T(8,128)}) custom-call(s32[8,1024]{1,0:T(8,128)S(1)} %get-tuple-element.12.place_ref, f32[1024,8]{1,0:T(8,128)S(1)} %bitcast.46, f32[30,512]{1,0:T(8,128)S(1)} %get-tuple-element.16.carried_ref, bf16[4,1536,512]{2,1,0:T(8,128)(2,1)S(1)} %bitcast.40, ...), custom_call_target="tpu_custom_call", output_to_operand_aliasing={{0}: (8, {})} | custom-call | flops 3221225472 | bytes 25165824 | tf_op jit(solution)/shard_map/stage/pallas_call | solution.py:244
  (13 shorter events, 0.0 us)
Async XLA Ops:
  6.5 1.0 copy-start
  6.5 54.2 %copy-start.7 = (s32[1,1024,8]{1,2,0:T(8,128)S(1)}, s32[1,1024,8]{1,2,0:T(8,128)}, u32[]{:S(2)}) copy-start(s32[1,1024,8]{1,2,0:T(8,128)} %param.11) | copy-start | bytes 98308
  6.5 54.2 %copy-start.6 = (s32[1,1024,8]{1,2,0:T(8,128)S(1)}, s32[1,1024,8]{1,2,0:T(8,128)}, u32[]{:S(2)}) copy-start(s32[1,1024,8]{1,2,0:T(8,128)} %param.10) | copy-start | bytes 98308
  6.5 49.9 %all-gather.3.cloned.1.call-start = ((), (), s32[]{:S(2)}) async-start(), calls=%async_computation.4 | async-start | bytes 1769472 | tf_op jit(solution)/shard_map/all_gather | solution.py:161
  59.2 35.8 %collective-permute-start.1 = (bf16[8,2,96,512]{3,2,0,1:T(8,128)(2,1)}, bf16[8,2,96,512]{3,2,0,1:T(8,128)(2,1)}, u32[]{:S(2)}, u32[]{:S(2)}) collective-permute-start(bf16[8,2,96,512]{3,2,0,1:T(8,128)(2,1)} %copy.24), channel_id=1, source_target_pairs={{0,1},{1,0},{2,3},{3,2},{4,5},{5,4},{6,7},{7,6},{8,9},{9,8},{10,11... | collective-permute-start | bytes 4718600 | tf_op jit(solution)/shard_map/ppermute | solution.py:162
  62.6 10.3 %all-to-all-start = ((s32[16,1,768]{2,1,0:T(1,128)}), s32[16,1,768]{2,1,0:T(1,128)S(1)}, u32[]{:S(2)}, u32[]{:S(2)}) async-start(s32[16,1,768]{2,1,0:T(1,128)} %copy.27), calls=%async_computation | async-start | bytes 98304 | tf_op jit(solution)/shard_map/all_to_all | solution.py:205
  72.9 2.2 %copy-start.1 = (f32[4,2048,128]{2,1,0:T(8,128)S(1)}, f32[4,2048,128]{2,1,0:T(8,128)}, u32[]{:S(2)}) copy-start(f32[4,2048,128]{2,1,0:T(8,128)} %reshape.56) | copy-start | bytes 12582916
  82.0 26.6 %all-to-all-start.1 = ((bf16[16,256,128]{2,1,0:T(8,128)(2,1)}), bf16[16,256,128]{2,1,0:T(8,128)(2,1)S(1)}, u32[]{:S(2)}, u32[]{:S(2)}) async-start(bf16[16,256,128]{2,1,0:T(8,128)(2,1)} %owner_gather.3), calls=%async_computation.1 | async-start | bytes 2097152 | tf_op jit(solution)/shard_map/all_to_all | solution.py:223
  97.2 2.4 %copy-start.9 = (bf16[8,2,96,512]{3,2,0,1:T(8,128)(2,1)}, bf16[8,2,96,512]{3,2,0,1:T(8,128)(2,1)S(1)}, u32[]{:S(2)}) copy-start(bf16[8,2,96,512]{3,2,0,1:T(8,128)(2,1)S(1)} %get-tuple-element.21) | copy-start | bytes 4718596
  97.2 3.2 %copy-start.10 = (bf16[8,2,96,512]{3,2,0,1:T(8,128)(2,1)}, bf16[8,2,96,512]{3,2,0,1:T(8,128)(2,1)S(1)}, u32[]{:S(2)}) copy-start(bf16[8,2,96,512]{3,2,0,1:T(8,128)(2,1)S(1)} %get-tuple-element.22) | copy-start | bytes 4718596
  97.2 4.5 %copy-start.2 = (f32[4,2048,128]{2,1,0:T(8,128)S(1)}, f32[4,2048,128]{2,1,0:T(8,128)}, u32[]{:S(2)}) copy-start(f32[4,2048,128]{2,1,0:T(8,128)} %reshape.56) | copy-start | bytes 12582916
  100.4 54.5 %collective-permute-start.2 = (bf16[8,4,96,512]{3,2,0,1:T(8,128)(2,1)}, bf16[8,4,96,512]{3,2,0,1:T(8,128)(2,1)}, u32[]{:S(2)}, u32[]{:S(2)}) collective-permute-start(bf16[8,4,96,512]{3,2,0,1:T(8,128)(2,1)} %pad_maximum_fusion.1), channel_id=1, source_target_pairs={{0,2},{2,0},{4,6},{6,4},{8,10},{10,8},{12,14},{14,12},{16,18},{18,... | collective-permute-start | bytes 9437192 | tf_op jit(solution)/shard_map/ppermute | solution.py:166
  108.6 29.7 %all-to-all-start.2 = ((bf16[16,256,128]{2,1,0:T(8,128)(2,1)}), bf16[16,256,128]{2,1,0:T(8,128)(2,1)S(1)}, u32[]{:S(2)}, u32[]{:S(2)}) async-start(bf16[16,256,128]{2,1,0:T(8,128)(2,1)} %owner_gather.4), calls=%async_computation.2 | async-start | bytes 2097152 | tf_op jit(solution)/shard_map/all_to_all | solution.py:223
  115.4 2.2 %copy-start.3 = (f32[4,2048,128]{2,1,0:T(8,128)S(1)}, f32[4,2048,128]{2,1,0:T(8,128)}, u32[]{:S(2)}) copy-start(f32[4,2048,128]{2,1,0:T(8,128)} %reshape.56) | copy-start | bytes 12582916
  117.6 27.7 %copy-start.11 = (bf16[8,30,512]{2,0,1:T(8,128)(2,1)S(1)}, bf16[8,30,512]{2,0,1:T(8,128)(2,1)}, u32[]{:S(2)}) copy-start(bf16[8,30,512]{2,0,1:T(8,128)(2,1)} %param.17) | copy-start | bytes 737284
  117.6 30.4 %copy-start.12 = (f32[1,1024,8]{1,2,0:T(8,128)S(1)}, f32[1,1024,8]{1,2,0:T(8,128)}, u32[]{:S(2)}) copy-start(f32[1,1024,8]{1,2,0:T(8,128)} %param.12) | copy-start | bytes 98308
  138.3 36.4 %all-to-all-start.3 = ((bf16[16,256,128]{2,1,0:T(8,128)(2,1)}), bf16[16,256,128]{2,1,0:T(8,128)(2,1)}, u32[]{:S(2)}, u32[]{:S(2)}) async-start(bf16[16,256,128]{2,1,0:T(8,128)(2,1)} %owner_gather.5), calls=%async_computation.3 | async-start | bytes 2097152 | tf_op jit(solution)/shard_map/all_to_all | solution.py:223
  145.4 8.7 %collective-permute-start = (bf16[8,30,512]{2,1,0:T(8,128)(2,1)S(1)}, bf16[8,30,512]{2,1,0:T(8,128)(2,1)}, u32[]{:S(2)}, u32[]{:S(2)}) collective-permute-start(bf16[8,30,512]{2,1,0:T(8,128)(2,1)S(1)} %copy.21), channel_id=1, source_target_pairs={{0,1},{1,0},{2,3},{3,2},{4,5},{5,4},{6,7},{7,6},{8,9},{9,8},{10,11... | collective-permute-start | bytes 737288 | tf_op jit(solution)/shard_map/ppermute | solution.py:232
  157.9 0.7 copy-start.8
  158.5 8.1 %copy-start.4 = (bf16[8,2,4,96,512]{4,3,1,0,2:T(8,128)(2,1)}, bf16[8,2,4,96,512]{4,3,1,0,2:T(8,128)(2,1)S(1)}, u32[]{:S(2)}) copy-start(bf16[8,2,4,96,512]{4,3,1,0,2:T(8,128)(2,1)S(1)} %pad_maximum_fusion) | copy-start | bytes 18874372
  174.8 2.8 %copy-start.5 = (bf16[8,2,4,96,512]{4,3,1,0,2:T(8,128)(2,1)S(1)}, bf16[8,2,4,96,512]{4,3,1,0,2:T(8,128)(2,1)}, u32[]{:S(2)}) copy-start(bf16[8,2,4,96,512]{4,3,1,0,2:T(8,128)(2,1)} %copy-done.4) | copy-start | bytes 18874372
Sparse Core Ops, SparseCore 0:
  9.5 46.8 all-gather.2
